TPU v7x, 32 devices: a whole 2x2x4 slice. The times are simulated.
32 devices in a mesh: groups: 2 (over y), pass: 4 (over z), cent: 2 (over x), rep: 2 (over core).
Axes of the slice: x: 2, y: 2, z: 4, core: 2. Of those that a mesh axis runs over, the one named last changes fastest.
Arguments:
- queries: bfloat16 [32, 32, 128], P(('groups', 'pass', 'cent', 'rep')), parts along dimension 0, may hold values from -6 to 6
- candidates: int32 [32, 64], P(('groups', 'pass', 'cent', 'rep')), parts along dimension 0, may hold values from 0 to 127, as said below
- residuals: bfloat16 [256, 128, 128], P(('groups', 'pass', 'cent')), parts along dimension 0, may hold values from -0.8984375 to 0.8984375
- centre_ids: int32 [256, 128], P(('groups', 'pass', 'cent')), parts along dimension 0, may hold values from 0 to 16383, as said below
- lengths: int32 [256], P(('groups', 'pass', 'cent')), parts along dimension 0, may hold values from 8 to 128
- centroids: bfloat16 [16384, 128], P(('pass', 'cent')), may hold values from -0.5 to 0.5
Outputs:
- centre_best: float32 [32, 32], P(('groups', 'pass', 'cent', 'rep')), parts along dimension 0
- scores: float32 [32, 64], P(('groups', 'pass', 'cent', 'rep')), parts along dimension 0
There are 2 independent parts, one for each index of `groups`. A program takes and returns all parts, laid end to end along the dimension named above; an argument that names none is the same for every part. Nothing has to cross between parts.
Inputs may be any that keep to these rules, and one draw needn't show every extreme that they name: `candidates`: passage p is held by index p // 16 of pass and cent. Among the candidate entries of the queries of one rep index, at most 192 name passages of one holder, and exactly 192 do for some holders. Entries of one query may repeat. `centre_ids`: centre c is held by index c // 2048 of pass and cent. The tokens of the passages of one holder name centres of each holder exactly 16 * 128 / 8 times.
All inputs are finite; a program needn't handle non-finite values.
Results may differ from a plain program's by a relative error of at most 0.00031.
Values may be sent and summed in bfloat16 or wider, within the bound.
A program may use at most 64 MiB of HBM per device.

v0:
```python
import math

import jax
import jax.numpy as jnp
from jax import lax
from jax.sharding import PartitionSpec as P


def on_device(queries, candidates, residuals, centre_ids, lengths, centroids):
    q_dev, qt, dim = queries.shape
    kc = candidates.shape[1]
    held, slots = (residuals.shape[0], residuals.shape[1])
    centres_here = centroids.shape[0]
    holders = lax.axis_size(("pass", "cent"))
    me = lax.axis_index(("pass", "cent"))
    flat_ids = centre_ids.reshape(-1)
    target = flat_ids // centres_here
    order = jnp.argsort(target, stable=True)
    each = flat_ids.shape[0] // holders
    requests = flat_ids[order].reshape(holders, each)
    found = centroids[
        lax.all_to_all(requests, ("pass", "cent"), split_axis=0, concat_axis=0, tiled=True)
        - me * centres_here
    ]
    arrived = lax.all_to_all(found, ("pass", "cent"), split_axis=0, concat_axis=0, tiled=True)
    inverse = jnp.zeros_like(order).at[order].set(jnp.arange(order.shape[0], dtype=jnp.int32))
    fetched = arrived.reshape(-1, dim)[inverse].reshape(held, slots, dim)
    gathered, cand_all = (
        lax.all_gather(queries, ("pass", "cent"), axis=0, tiled=True),
        lax.all_gather(candidates, ("pass", "cent"), axis=0, tiled=True),
    )
    half = gathered.shape[0]
    tokens = gathered.reshape(-1, dim)
    block = math.gcd(tokens.shape[0], 1024)

    def centre_max(rows):
        return jnp.max(
            jnp.einsum("td,cd->tc", rows, centroids, preferred_element_type=jnp.float32), axis=1
        )

    local_max = lax.map(centre_max, tokens.reshape(-1, block, dim)).reshape(half, qt)
    flat = cand_all.reshape(-1) - me * held
    mine = (flat >= 0) & (flat < held)
    slot_of = jnp.cumsum(mine.astype(jnp.int32)) - 1
    capacity = 3 * q_dev * kc
    spot_of = jnp.where(mine, slot_of, capacity)
    entry = (
        jnp.zeros((capacity,), jnp.int32)
        .at[spot_of]
        .set(jnp.arange(flat.shape[0], dtype=jnp.int32), mode="drop")
    )
    valid = jnp.arange(capacity, dtype=jnp.int32) < jnp.sum(mine.astype(jnp.int32))
    query_row = entry // kc
    passage_row = jnp.clip(flat[entry], 0, held - 1)
    q_rows = gathered[query_row]
    decoded = (fetched.astype(jnp.float32) + residuals.astype(jnp.float32)).astype(jnp.bfloat16)
    p_rows = decoded[passage_row]
    sims = jnp.einsum("sqd,spd->sqp", q_rows, p_rows, preferred_element_type=jnp.float32)
    live = jnp.arange(slots, dtype=jnp.int32)[None, :] < lengths[passage_row][:, None]
    best = jnp.max(jnp.where(live[:, None, :], sims, -jnp.inf), axis=2)
    pair_value = jnp.where(valid, jnp.sum(best, axis=1) / qt, 0.0)
    spot = jnp.where(valid, entry, half * kc)
    term = (
        jnp.zeros((half * kc,), jnp.float32).at[spot].set(pair_value, mode="drop").reshape(half, kc)
    )
    maxima = lax.pmax(local_max, ("pass", "cent"))
    centre_best = lax.dynamic_slice_in_dim(maxima, me * q_dev, q_dev, 0)
    scores = lax.psum_scatter(term, ("pass", "cent"), scatter_dimension=0, tiled=True)
    return (centre_best, scores)


def solution(mesh):
    return jax.shard_map(
        on_device,
        mesh=mesh,
        in_specs=(
            P(("groups", "pass", "cent", "rep"), None, None),
            P(("groups", "pass", "cent", "rep"), None),
            P(("groups", "pass", "cent"), None, None),
            P(("groups", "pass", "cent"), None),
            P(("groups", "pass", "cent")),
            P(("pass", "cent"), None),
        ),
        out_specs=(
            P(("groups", "pass", "cent", "rep"), None),
            P(("groups", "pass", "cent", "rep"), None),
        ),
        check_vma=False,
    )
```

profile of v0, /device:TPU:0, one launch (start us, length us, event | category | flops | bytes accessed | tf_op | source)
XLA Modules:
  0.0 188.9 jit_solution(9096459791778158425)
XLA Ops:
  0.7 0.8 add_select_fusion
  1.4 5.0 %sort.17 = (s32[2048]{0:T(1024)}, s32[2048]{0:T(1024)S(1)}) sort(s32[2048]{0:T(1024)S(1)} %add_select_fusion, s32[2048]{0:T(1024)S(1)} %iota.22), dimensions={0}, to_apply=%region_6.7 | sort | flops 22528 | bytes 32768 | tf_op jit(solution)/shard_map/jit(argsort)/sort | solution.py:18
  6.5 20.6 %gather_fusion.2 = s32[2048]{0:T(1024)} fusion(s32[2048]{0:T(1024)S(1)} %bitcast.37, s32[2048]{0:T(1024)S(1)} %get-tuple-element.20), kind=kCustom, calls=%fused_computation.2 | custom fusion | bytes 24576 | tf_op jit(solution)/shard_map/gather | solution.py:20
  27.1 7.3 %all-to-all-start = ((s32[8,1,256]{2,1,0:T(1,128)}), s32[8,1,256]{2,1,0:T(1,128)S(1)}, u32[]{:S(2)}, u32[]{:S(2)}) async-start(s32[8,1,256]{2,1,0:T(1,128)} %bitcast.23), calls=%async_computation | async-start | bytes 16384 | tf_op jit(solution)/shard_map/all_to_all | solution.py:22
  34.3 20.9 %all-gather = s32[8,1,64]{2,1,0:T(1,128)S(1)} all-gather(s32[1,1,64]{2,1,0:T(1,128)S(1)} %bitcast.47), channel_id=1, replica_groups=mesh['groups'=2,'pass'=4,'cent'=2,'rep'=2] {'pass','cent'}, dimensions={0}, use_global_device_ids=true | all-gather | bytes 2304 | tf_op jit(solution)/shard_map/all_gather | solution.py:30
  56.6 2.4 %scatter_custom_fusion = s32[192]{0:T(256)S(1)} fusion(s32[512]{0:T(512)S(1)} %bitcast.46, s32[512]{0:T(512)S(1)} %iota.21, s32[]{:T(128)} %constant.40.clone.1), kind=kCustom, calls=%fused_computation.68 | custom fusion | bytes 772 | tf_op jit(solution)/shard_map/scatter | solution.py:50
  59.1 0.7 add_select_fusion.1
  59.8 1.6 gather_fusion
  61.5 30.5 %all_gather.6 = bf16[8,32,128]{2,1,0:T(8,128)(2,1)S(1)} all-gather(bf16[1,32,128]{2,1,0:T(8,128)(2,1)S(1)} %copy-done.3), channel_id=1, replica_groups=mesh['groups'=2,'pass'=4,'cent'=2,'rep'=2] {'pass','cent'}, dimensions={0}, use_global_device_ids=true | all-gather | bytes 73728 | tf_op jit(solution)/shard_map/all_gather | solution.py:29
  92.6 17.1 %pmax.7 = f32[8,32]{1,0:T(8,128)S(1)} all-reduce(f32[8,32]{1,0:T(8,128)S(1)} %reshape.170), channel_id=1, replica_groups=mesh['groups'=2,'pass'=4,'cent'=2,'rep'=2] {'pass','cent'}, use_global_device_ids=true, to_apply=%region_1.2 | all-reduce | flops 256 | bytes 2048 | tf_op jit(solution)/shard_map/pmax | solution.py:66
  109.8 8.0 %gather_fusion.3 = bf16[2048,128]{1,0:T(8,128)(2,1)} fusion(bf16[2048,128]{1,0:T(8,128)(2,1)S(1)} %copy-done, s32[2048]{0:T(1024)S(1)} %broadcast_clamp_fusion.1), kind=kCustom, calls=%fused_computation.3 | custom fusion | bytes 1056768 | tf_op jit(solution)/shard_map/gather | solution.py:21
  117.7 3.6 %all-to-all-start.1 = ((bf16[8,256,128]{2,1,0:T(8,128)(2,1)}), bf16[8,256,128]{2,1,0:T(8,128)(2,1)S(1)}, u32[]{:S(2)}, u32[]{:S(2)}) async-start(bf16[8,256,128]{2,1,0:T(8,128)(2,1)} %bitcast.26), calls=%async_computation.1 | async-start | bytes 1048576 | tf_op jit(solution)/shard_map/all_to_all | solution.py:25
  121.9 0.9 gather_fusion.1
  122.8 8.2 %scatter_custom_fusion.1 = s32[2048]{0:T(1024)S(1)} fusion(s32[2048]{0:T(1024)S(1)} %get-tuple-element.19, s32[2048]{0:T(1024)S(1)} %iota.23, s32[]{:T(128)} %constant.40.clone.1), kind=kCustom, calls=%fused_computation.35 | custom fusion | bytes 8196 | tf_op jit(solution)/shard_map/scatter | solution.py:26
  131.7 0.7 fusion.10
  132.4 9.9 %compare_select_fusion.7 = s32[192]{0:T(256)S(1)} fusion(s32[192]{0:T(256)S(1)} %bitcast.43, s32[]{:T(128)} %bitcast.6, s32[]{:T(128)} %bitcast.7, s32[]{:T(128)} %bitcast.8, s32[]{:T(128)} %bitcast.9, s32[]{:T(128)} %bitcast.10, s32[]{:T(128)} %bitcast.11, s32[]{:T(128)} %bitcast.12, s32[]{:T(128)} %bitcast.13, s32[]{:T(128)} %bitcast.14, s32[]{:T(128)} %bitcast.15, ...), kind=kLoop, calls=%fused_computation.42 | loop fusion | flops 5760 | bytes 1600 | tf_op jit(solution)/shard_map/gather | solution.py:59
  142.4 6.2 %gather_fusion.4 = bf16[2048,128]{1,0:T(8,128)(2,1)S(1)} fusion(bf16[2048,128]{1,0:T(8,128)(2,1)S(1)} %bitcast.38, s32[2048]{0:T(1024)S(1)} %fusion.2), kind=kCustom, calls=%fused_computation.4 | custom fusion | bytes 1056768 | tf_op jit(solution)/shard_map/gather | solution.py:27
  148.6 1.2 fusion
  149.8 8.0 %gather_fusion.5 = bf16[192,128,128]{2,1,0:T(8,128)(2,1)} fusion(bf16[16,128,128]{2,1,0:T(8,128)(2,1)S(1)} %fusion, s32[1024]{0:T(1024)S(1)} %pad_clamp_fusion), kind=kCustom, calls=%fused_computation.5 | custom fusion | bytes 12583680 | tf_op jit(solution)/shard_map/gather | solution.py:57
  157.7 6.2 %select_reduce_fusion = f32[192,32]{1,0:T(8,128)S(1)} fusion(bf16[192,32,128]{2,1,0:T(8,128)(2,1)S(1)} %gather_fusion.1, bf16[192,128,128]{2,1,0:T(8,128)(2,1)} %gather_fusion.5, pred[192,128]{1,0:T(8,128)(4,1)S(1)} %iota_compare_fusion), kind=kOutput, calls=%fused_computation.9 | convolution fusion | flops 202893312 | bytes 7913472 | tf_op jit(solution)/shard_map/sqd,spd->sqp/dot_general | solution.py:58
  164.1 0.7 multiply_select_fusion
  164.8 1.2 scatter_custom_fusion.2
  166.1 21.8 %all-reduce = f32[8,64]{1,0:T(8,128)S(1)} all-reduce(f32[8,64]{1,0:T(8,128)S(1)} %reshape.174), channel_id=2, replica_groups=mesh['groups'=2,'pass'=4,'cent'=2,'rep'=2] {'pass','cent'}, use_global_device_ids=true, to_apply=%region_11.12.clone | all-reduce | flops 512 | bytes 4096
  187.8 1.1 constant_dynamic-slice_fusion
  (44 shorter events, 3.6 us)
Async XLA Ops:
  0.6 91.3 %copy-start = (bf16[2048,128]{1,0:T(8,128)(2,1)S(1)}, bf16[2048,128]{1,0:T(8,128)(2,1)}, u32[]{:S(2)}) copy-start(bf16[2048,128]{1,0:T(8,128)(2,1)} %param.11) | copy-start | bytes 1572868
  0.6 5.8 %copy-start.1 = (s32[16,128]{1,0:T(8,128)S(1)}, s32[16,128]{1,0:T(8,128)}, u32[]{:S(2)}) copy-start(s32[16,128]{1,0:T(8,128)} %param.9) | copy-start | bytes 24580
  6.5 27.8 %copy-start.4 = (s32[1,64]{1,0:T(1,128)S(1)}, s32[1,64]{1,0:T(1,128)}, u32[]{:S(2)}) copy-start(s32[1,64]{1,0:T(1,128)} %param.7) | copy-start | bytes 772
  6.5 55.0 %copy-start.3 = (bf16[1,32,128]{2,1,0:T(8,128)(2,1)S(1)}, bf16[1,32,128]{2,1,0:T(8,128)(2,1)}, u32[]{:S(2)}) copy-start(bf16[1,32,128]{2,1,0:T(8,128)(2,1)} %param.6) | copy-start | bytes 24580
  27.1 82.7 %all-to-all-start = ((s32[8,1,256]{2,1,0:T(1,128)}), s32[8,1,256]{2,1,0:T(1,128)S(1)}, u32[]{:S(2)}, u32[]{:S(2)}) async-start(s32[8,1,256]{2,1,0:T(1,128)} %bitcast.23), calls=%async_computation | async-start | bytes 16384 | tf_op jit(solution)/shard_map/all_to_all | solution.py:22
  117.7 13.3 %copy-start.5 = (u32[32]{0:T(128)S(1)}, u32[32]{0:T(128)}, u32[]{:S(2)}) copy-start(u32[32]{0:T(128)} %constant.107) | copy-start | bytes 388
  117.7 13.9 %copy-start.2 = (s32[16]{0:T(128)S(1)}, s32[16]{0:T(128)}, u32[]{:S(2)}) copy-start(s32[16]{0:T(128)} %param.10) | copy-start | bytes 196
  117.7 24.6 %all-to-all-start.1 = ((bf16[8,256,128]{2,1,0:T(8,128)(2,1)}), bf16[8,256,128]{2,1,0:T(8,128)(2,1)S(1)}, u32[]{:S(2)}, u32[]{:S(2)}) async-start(bf16[8,256,128]{2,1,0:T(8,128)(2,1)} %bitcast.26), calls=%async_computation.1 | async-start | bytes 1048576 | tf_op jit(solution)/shard_map/all_to_all | solution.py:25
where the time goes:
time: 189 us
  blocking collectives  90.3 us (48%)
  local copies, waits for them, and re-layouts  60.6 us (32%)
  other arithmetic  19.6 us (10%)
  starting transfers between devices  10.9 us (6%)
  matrix products  6.75 us (4%)
    all_gather x1, blocking collectives, on_device(): lax.all_gather(queries, ('pass', 'cent'), axis=0, tiled=True)  30.5 us
    unnamed x1, blocking collectives  21.8 us
    all_gather x1, blocking collectives, on_device(): lax.all_gather(candidates, ('pass', 'cent'), axis=0, tiled=True)  20.9 us
    gather x1, local copies, waits for them, and re-layouts, on_device(): requests = flat_ids[order].reshape(holders, each)  20.6 us
    pmax x1, blocking collectives, on_device(): maxima = lax.pmax(local_max, ('pass', 'cent'))  17.1 us
    gather x1, other arithmetic, on_device(): lengths[passage_row][:, None]  9.88 us
    scatter x1, local copies, waits for them, and re-layouts, on_device(): jnp.zeros_like(order).at[order]  8.23 us
    gather x1, local copies, waits for them, and re-layouts, on_device(): p_rows = decoded[passage_row]  7.98 us
  transfers between devices with their start and end apart: 2, of which 0 were waited for; matrix products, arithmetic and copies ran while one was open for 15% of the time, Pallas kernels for 0%

commit v1 on v0

--- a/solution.py
+++ b/solution.py
@@ -1,12 +1,272 @@
+import functools
 import math
 
 import jax
 import jax.numpy as jnp
 from jax import lax
+from jax.experimental import pallas as pl
+from jax.experimental.pallas import tpu as pltpu
 from jax.sharding import PartitionSpec as P
 
-
-def on_device(queries, candidates, residuals, centre_ids, lengths, centroids):
+MESH = pl.DeviceIdType.MESH
+NT = (((1,), (1,)), ((), ()))
+F32 = jnp.float32
+BF16 = jnp.bfloat16
+
+
+def iota(shape, axis):
+    return lax.broadcasted_iota(jnp.int32, shape, axis)
+
+
+def ones_where(mask):
+    return jnp.where(mask, 1.0, 0.0).astype(BF16)
+
+
+def log2(n):
+    return n.bit_length() - 1
+
+
+def fused_kernel(
+    holders, n_cent,
+    q_ref, cand_ref, res_ref, ids_ref, len_ref, cent_ref,
+    best_ref, score_ref,
+    q_all, req_out, req_in, found, rows, stat_out, stat_in, slot_ref, pick, pair_max,
+    q_send, q_recv, r_send, r_recv, f_send, f_recv, x_send, x_recv, s_send, s_recv,
+):
+    qt, dim = q_ref.shape
+    held, slots = ids_ref.shape
+    centres = cent_ref.shape[0]
+    half = rows.shape[2]
+    me = lax.axis_index("pass") * n_cent + lax.axis_index("cent")
+    rep = lax.axis_index("rep")
+
+    def at(step):
+        h = lax.rem(me + step + holders, holders)
+        return {"pass": lax.div(h, n_cent), "cent": lax.rem(h, n_cent)}
+
+    other = {"rep": 1 - rep}
+    far_first = sorted(range(1, holders), key=lambda k: -min(k, holders - k))
+
+    barrier = pltpu.get_barrier_semaphore()
+    for k in range(1, holders):
+        pl.semaphore_signal(barrier, inc=1, device_id=at(k), device_id_type=MESH)
+    pl.semaphore_signal(barrier, inc=1, device_id=other, device_id_type=MESH)
+
+    ids = ids_ref[...]
+    target = ((ids >> log2(centres)) - me) & (holders - 1)
+    local_id = ids & (centres - 1)
+    masks = [jnp.where(target == k, 1.0, 0.0) for k in range(holders)]
+    mask = jnp.concatenate(masks, axis=0).astype(BF16)
+    rows_of = holders * held
+    before = ones_where(iota((slots, slots), 0) < iota((slots, slots), 1))
+    in_row = jnp.dot(mask, before, preferred_element_type=F32)
+    total = jnp.dot(mask, jnp.ones((slots, slots), BF16), preferred_element_type=F32)
+    a, b = iota((rows_of, rows_of), 0), iota((rows_of, rows_of), 1)
+    above = ones_where(((a >> log2(held)) == (b >> log2(held))) & (b < a))
+    rank_all = in_row + jnp.dot(above, total.astype(BF16), preferred_element_type=F32)
+    rank = jnp.zeros((held, slots), F32)
+    for k in range(holders):
+        rank = rank + masks[k] * rank_all[k * held : (k + 1) * held]
+    slot_ref[...] = target.astype(F32) * (2.0 * half) + rank
+
+    low = (local_id & 255).astype(F32)
+    high = (local_id >> 8).astype(F32)
+    shifted = rank - (rep * half).astype(F32)
+    by_rank = iota((half, slots), 0).astype(F32)
+    by_holder = iota((holders, slots), 0)
+    asked = jnp.zeros((2 * holders, half), F32)
+    for p in range(held):
+        at_rank = ones_where(shifted[p : p + 1] == by_rank)
+        named = target[p : p + 1] == by_holder
+        parts = jnp.concatenate(
+            [jnp.where(named, low[p : p + 1], 0.0), jnp.where(named, high[p : p + 1], 0.0)], axis=0
+        ).astype(BF16)
+        asked = asked + lax.dot_general(parts, at_rank, NT, preferred_element_type=F32)
+    asked = (asked[:holders] + 256.0 * asked[holders:]).astype(jnp.int32)
+    for k in range(1, holders):
+        req_out[k] = jnp.broadcast_to(asked[k : k + 1], (8, half))
+    req_in[0] = jnp.broadcast_to(asked[0:1], (8, half))
+    q_all[0] = q_ref[...]
+    stat_out[...] = jnp.zeros_like(stat_out)
+
+    pl.semaphore_wait(barrier, holders)
+
+    def remote(src, dst, send, recv, device):
+        return pltpu.make_async_remote_copy(
+            src_ref=src, dst_ref=dst, send_sem=send, recv_sem=recv,
+            device_id=device, device_id_type=MESH,
+        )
+
+    def req_copy(k):
+        return remote(req_out.at[k], req_in.at[k], r_send.at[k], r_recv.at[k], at(k))
+
+    def q_copy(k):
+        return remote(q_ref, q_all.at[k], q_send.at[k], q_recv.at[k], at(k))
+
+    def row_copy(k):
+        return remote(found.at[k], rows.at[k, rep], f_send.at[k], f_recv.at[k], at(-k))
+
+    def swap_copy(k):
+        return remote(rows.at[k, rep], rows.at[k, rep], x_send.at[k], x_recv.at[k], other)
+
+    def swap_arrival(k):
+        return remote(rows.at[k, rep], rows.at[k, 1 - rep], x_send.at[k], x_recv.at[k], other)
+
+    def stat_copy(k):
+        return remote(stat_out, stat_in.at[k], s_send.at[k], s_recv.at[k], at(-k))
+
+    for k in far_first:
+        req_copy(k).start()
+    for k in far_first:
+        q_copy(k).start()
+
+    lanes = iota((half, 128), 1)
+
+    def across(row):
+        return jnp.transpose(jnp.broadcast_to(row, (half, half)))
+
+    def chosen(row, width):
+        spread = across(row)
+        return jnp.concatenate(
+            [ones_where(spread - j * 128.0 == lanes.astype(F32)) for j in range(width // 128)], axis=1
+        )
+
+    for k in far_first + [0]:
+        if k:
+            req_copy(k).wait_recv()
+        hit = chosen(req_in[k][0:1].astype(F32), centres)
+        got = jnp.dot(hit, cent_ref[...], preferred_element_type=F32).astype(BF16)
+        if k:
+            found[k] = got
+            row_copy(k).start()
+        else:
+            rows[0, rep] = got
+            swap_copy(0).start()
+
+    for k in far_first:
+        q_copy(k).wait_recv()
+    tokens = q_all[...].reshape(holders * qt, dim)
+    best = None
+    for j in range(centres // 256):
+        part = lax.dot_general(
+            cent_ref[j * 256 : (j + 1) * 256], tokens, NT, preferred_element_type=F32
+        )
+        best = part if best is None else jnp.maximum(best, part)
+    best = jnp.max(best, axis=0, keepdims=True)
+    width = holders * qt
+    own = (iota((holders, width), 1) >> log2(qt)) == iota((holders, width), 0)
+    fold = jnp.where((iota((width, 128), 0) & (qt - 1)) == iota((width, 128), 1), 1.0, 0.0)
+    stat_out[holders : 2 * holders] = jnp.dot(
+        jnp.where(own, best, 0.0), fold, precision=lax.Precision.HIGHEST, preferred_element_type=F32
+    )
+
+    def choose(p, _):
+        row = slot_ref[pl.ds(p, 1), :]
+        pick[p] = chosen(row, 2 * half * holders)
+        return 0
+
+    lax.fori_loop(0, held, choose, 0)
+
+    near_first = far_first[::-1]
+    for k in near_first:
+        row_copy(k).wait_recv()
+        swap_copy(k).start()
+    for k in [0] + near_first:
+        swap_arrival(k).wait_recv()
+
+    step = math.gcd(held, 4)
+    centre_rows = rows[...].reshape(holders * 2 * half, dim)
+    spot = iota((slots, width), 0)
+    for g in range(held // step):
+        group = pick[g * step : (g + 1) * step].reshape(step * slots, 2 * half * holders)
+        fetched = jnp.dot(group, centre_rows, preferred_element_type=F32)
+        residual = res_ref[g * step : (g + 1) * step].reshape(step * slots, dim).astype(F32)
+        decoded = (fetched + residual).astype(BF16)
+        sims = lax.dot_general(decoded, tokens, NT, preferred_element_type=F32)
+        for i in range(step):
+            p = g * step + i
+            live = jnp.where(spot < len_ref[p], sims[i * slots : (i + 1) * slots], -jnp.inf)
+            pair_max[p : p + 1] = jnp.max(live, axis=0, keepdims=True)
+    seg = jnp.where(own, 1.0, 0.0)
+    table = lax.dot_general(
+        seg, pair_max[...], NT, precision=lax.Precision.HIGHEST, preferred_element_type=F32
+    )
+    stat_out[0:holders, 0:held] = table / qt
+
+    for k in far_first:
+        stat_copy(k).start()
+    for k in far_first:
+        stat_copy(k).wait_recv()
+
+    picked = [stat_out[0:1, 0:held]] + [stat_in[k][k : k + 1, 0:held] for k in range(1, holders)]
+    maxima = stat_out[holders : holders + 1]
+    for k in range(1, holders):
+        maxima = jnp.maximum(maxima, stat_in[k][holders + k : holders + k + 1])
+    best_ref[...] = maxima[:, 0:qt]
+    table = jnp.concatenate(picked, axis=0)
+    cand = cand_ref[...]
+    kc = cand.shape[1]
+    where_p = jnp.where(iota((held, kc), 0) == (cand & (held - 1)), 1.0, 0.0)
+    value = jnp.dot(table, where_p, precision=lax.Precision.HIGHEST, preferred_element_type=F32)
+    holder = ((cand >> log2(held)) - me) & (holders - 1)
+    score_ref[...] = jnp.sum(
+        jnp.where(iota((holders, kc), 0) == holder, value, 0.0), axis=0, keepdims=True
+    )
+
+    for k in range(1, holders):
+        req_copy(k).wait_send()
+        q_copy(k).wait_send()
+        row_copy(k).wait_send()
+        stat_copy(k).wait_send()
+    for k in range(holders):
+        swap_copy(k).wait_send()
+
+
+def fused(queries, candidates, residuals, centre_ids, lengths, centroids):
+    q_dev, qt, dim = queries.shape
+    holders = lax.axis_size(("pass", "cent"))
+    held, slots = centre_ids.shape
+    half = held * slots // holders // 2
+    vmem = pl.BlockSpec(memory_space=pltpu.VMEM)
+    dma = lambda: pltpu.SemaphoreType.DMA((holders,))
+    return pl.pallas_call(
+        functools.partial(fused_kernel, holders, lax.axis_size("cent")),
+        out_shape=(
+            jax.ShapeDtypeStruct((q_dev, qt), F32),
+            jax.ShapeDtypeStruct((q_dev, candidates.shape[1]), F32),
+        ),
+        in_specs=[vmem, vmem, vmem, vmem, pl.BlockSpec(memory_space=pltpu.SMEM), vmem],
+        out_specs=(vmem, vmem),
+        scratch_shapes=[
+            pltpu.VMEM((holders, qt, dim), BF16),
+            pltpu.VMEM((holders, 8, half), jnp.int32),
+            pltpu.VMEM((holders, 8, half), jnp.int32),
+            pltpu.VMEM((holders, half, dim), BF16),
+            pltpu.VMEM((holders, 2, half, dim), BF16),
+            pltpu.VMEM((2 * holders, 128), F32),
+            pltpu.VMEM((holders, 2 * holders, 128), F32),
+            pltpu.VMEM((held, slots), F32),
+            pltpu.VMEM((held, slots, 2 * half * holders), BF16),
+            pltpu.VMEM((held, holders * qt), F32),
+        ]
+        + [dma() for _ in range(10)],
+        compiler_params=pltpu.CompilerParams(
+            collective_id=0, has_side_effects=True, vmem_limit_bytes=40 * 1024 * 1024
+        ),
+    )(queries.reshape(qt, dim), candidates, residuals, centre_ids, lengths, centroids)
+
+
+def fits(queries, residuals, centroids, holders, reps):
+    q_dev, qt, dim = queries.shape
+    held, slots = residuals.shape[:2]
+    powers = all(n & (n - 1) == 0 for n in (qt, held, holders, centroids.shape[0]))
+    return (
+        powers and q_dev == 1 and reps == 2 and dim == 128 and slots == 128 and holders == 8
+        and held * slots == 256 * holders and centroids.shape[0] % 256 == 0
+    )
+
+
+def on_device_large(queries, candidates, residuals, centre_ids, lengths, centroids):
     q_dev, qt, dim = queries.shape
     kc = candidates.shape[1]
     held, slots = (residuals.shape[0], residuals.shape[1])
@@ -69,6 +329,13 @@
     return (centre_best, scores)
 
 
+def on_device(queries, candidates, residuals, centre_ids, lengths, centroids):
+    args = (queries, candidates, residuals, centre_ids, lengths, centroids)
+    if fits(queries, residuals, centroids, lax.axis_size(("pass", "cent")), lax.axis_size("rep")):
+        return fused(*args)
+    return on_device_large(*args)
+
+
 def solution(mesh):
     return jax.shard_map(
         on_device,

time: 189 us -> 32.4 us (0.17)
  blocking collectives: 90.3 us -> 0 us
  local copies, waits for them, and re-layouts: 60.6 us -> 5.15 us
  Pallas kernels: 0 us -> 26.3 us
  other arithmetic: 19.6 us -> 0 us
  starting transfers between devices: 10.9 us -> 0 us
  matrix products: 6.75 us -> 0 us
    all_gather x2 -> x0, blocking collectives: 51.4 us -> none  [the longest x1 30.5 us: on_device(): lax.all_gather(queries, ('pass', 'cent'), axis=0, tiled=True)]
    gather x7 -> x0, local copies, waits for them, and re-layouts: 45.9 us -> none  [the longest x1 20.6 us: on_device(): requests = flat_ids[order].reshape(holders, each)]
    pallas_call x0 -> x1, Pallas kernels: none -> 26.3 us  [fused(): pl.pallas_call(functools.partial(fused_kernel, holders, lax.axis_size('ce...]
    unnamed x1 -> x0, blocking collectives: 21.8 us -> none
    pmax x1 -> x0, blocking collectives: 17.1 us -> none  [on_device(): maxima = lax.pmax(local_max, ('pass', 'cent'))]
    scatter x3 -> x0, local copies, waits for them, and re-layouts: 11.9 us -> none  [the longest x1 8.23 us: on_device(): jnp.zeros_like(order).at[order]]
    all_to_all x2 -> x0, starting transfers between devices: 10.9 us -> none  [the longest x1 7.25 us: on_device(): lax.all_to_all(requests, ('pass', 'cent'), split_axis=0, concat_axis=0, t...]
    gather x6 -> x0, other arithmetic: 9.91 us -> none  [the longest x1 9.88 us: on_device(): lengths[passage_row][:, None]]
  transfers between devices with their start and end apart: 2 -> 0, of which waited for: 0 -> 0; matrix products, arithmetic and copies ran while one was open for 15% -> 0% of each run, Pallas kernels for 0% -> 0%
where the time goes in v1:
time: 32.4 us; the launch traced here: 32.1 us
  Pallas kernels  26.3 us (81%)
  local copies, waits for them, and re-layouts  5.15 us (16%)
  between operations  0.66 us (2%)
    pallas_call x1, Pallas kernels, fused(): pl.pallas_call(functools.partial(fused_kernel, holders, lax.axis_size('ce...  26.3 us
    unnamed x14, local copies, waits for them, and re-layouts  5.15 us

profile of v1, /device:TPU:0, one launch (start us, length us, event | category | flops | bytes accessed | tf_op | source)
XLA Modules:
  0.0 32.1 jit_solution(17620108372232063175)
XLA Ops:
  0.6 0.0 copy-start.5
  0.6 0.0 copy-start.4
  0.7 0.6 %copy-done.5 = s32[16]{0:T(128)S(1)} copy-done((s32[16]{0:T(128)S(1)}, s32[16]{0:T(128)}, u32[]{:S(2)}) %copy-start.5) | copy-done | bytes 88
  1.3 0.0 copy-done.4
  1.3 0.0 copy-start
  1.3 1.0 %copy-done = bf16[16,128,128]{2,1,0:T(8,128)(2,1)S(1)} copy-done((bf16[16,128,128]{2,1,0:T(8,128)(2,1)S(1)}, bf16[16,128,128]{2,1,0:T(8,128)(2,1)}, u32[]{:S(2)}) %copy-start) | copy-done | bytes 524312
  2.3 0.0 copy-start.1
  2.3 1.0 %copy-done.1 = bf16[2048,128]{1,0:T(8,128)(2,1)S(1)} copy-done((bf16[2048,128]{1,0:T(8,128)(2,1)S(1)}, bf16[2048,128]{1,0:T(8,128)(2,1)}, u32[]{:S(2)}) %copy-start.1) | copy-done | bytes 524312
  3.4 0.0 copy-start.2
  3.4 0.7 %copy-done.2 = bf16[1,32,128]{2,1,0:T(8,128)(2,1)S(1)} copy-done((bf16[1,32,128]{2,1,0:T(8,128)(2,1)S(1)}, bf16[1,32,128]{2,1,0:T(8,128)(2,1)}, u32[]{:S(2)}) %copy-start.2) | copy-done | bytes 8216
  4.1 0.0 copy-start.3
  4.1 0.7 %copy-done.3 = s32[16,128]{1,0:T(8,128)S(1)} copy-done((s32[16,128]{1,0:T(8,128)S(1)}, s32[16,128]{1,0:T(8,128)}, u32[]{:S(2)}) %copy-start.3) | copy-done | bytes 8216
  4.8 26.3 %shard_map.77 = (f32[1,32]{1,0:T(1,128)S(1)}, f32[1,64]{1,0:T(1,128)S(1)}) custom-call(bf16[32,128]{1,0:T(8,128)(2,1)S(1)} %bitcast.1, s32[1,64]{1,0:T(1,128)S(1)} %copy-done.4, bf16[16,128,128]{2,1,0:T(8,128)(2,1)S(1)} %copy-done, s32[16,128]{1,0:T(8,128)S(1)} %copy-done.3, s32[16]{0:T(128)S(1)} %copy-done.5, bf16[2048,128]{1,0:T(8,128)(2,1)S(1)} %copy-done.1), custom_call_target="tpu_custom_call" | custom-call | tf_op jit(solution)/shard_map/pallas_call | solution.py:232
  31.1 0.5 %copy.10 = f32[1,32]{1,0:T(1,128)} copy(f32[1,32]{1,0:T(1,128)S(1)} %get-tuple-element.4) | data formatting | bytes 256
  31.6 0.5 %copy.11 = f32[1,64]{1,0:T(1,128)} copy(f32[1,64]{1,0:T(1,128)S(1)} %get-tuple-element.5) | data formatting | bytes 512
Async XLA Ops:
  0.6 0.7 %copy-start.5 = (s32[16]{0:T(128)S(1)}, s32[16]{0:T(128)}, u32[]{:S(2)}) copy-start(s32[16]{0:T(128)} %len_ref.1) | copy-start | bytes 196
  0.6 0.7 %copy-start.4 = (s32[1,64]{1,0:T(1,128)S(1)}, s32[1,64]{1,0:T(1,128)}, u32[]{:S(2)}) copy-start(s32[1,64]{1,0:T(1,128)} %cand_ref.1) | copy-start | bytes 772
  1.3 1.0 %copy-start = (bf16[16,128,128]{2,1,0:T(8,128)(2,1)S(1)}, bf16[16,128,128]{2,1,0:T(8,128)(2,1)}, u32[]{:S(2)}) copy-start(bf16[16,128,128]{2,1,0:T(8,128)(2,1)} %res_ref.1) | copy-start | bytes 1572868
  2.3 1.0 %copy-start.1 = (bf16[2048,128]{1,0:T(8,128)(2,1)S(1)}, bf16[2048,128]{1,0:T(8,128)(2,1)}, u32[]{:S(2)}) copy-start(bf16[2048,128]{1,0:T(8,128)(2,1)} %cent_ref.1) | copy-start | bytes 1572868
  3.4 0.7 %copy-start.2 = (bf16[1,32,128]{2,1,0:T(8,128)(2,1)S(1)}, bf16[1,32,128]{2,1,0:T(8,128)(2,1)}, u32[]{:S(2)}) copy-start(bf16[1,32,128]{2,1,0:T(8,128)(2,1)} %param.6) | copy-start | bytes 24580
  4.1 0.7 %copy-start.3 = (s32[16,128]{1,0:T(8,128)S(1)}, s32[16,128]{1,0:T(8,128)}, u32[]{:S(2)}) copy-start(s32[16,128]{1,0:T(8,128)} %ids_ref.1) | copy-start | bytes 24580

commit v2 on v1

--- a/solution.py
+++ b/solution.py
@@ -28,12 +28,13 @@
 
 def fused_kernel(
     holders, n_cent,
-    q_ref, cand_ref, res_ref, ids_ref, len_ref, cent_ref,
+    q_hbm, cand_hbm, res_hbm, ids_hbm, len_hbm, cent_hbm,
     best_ref, score_ref,
-    q_all, req_out, req_in, found, rows, stat_out, stat_in, slot_ref, pick, pair_max,
+    cand_ref, res_ref, ids_ref, len_ref, cent_ref, in_sem,
+    q_all, req_out, req_in, found, rows, stat_out, stat_in, slot_ref, later_ref, later_all, pick, pair_max, wide_cent,
     q_send, q_recv, r_send, r_recv, f_send, f_recv, x_send, x_recv, s_send, s_recv,
 ):
-    qt, dim = q_ref.shape
+    qt, dim = q_hbm.shape
     held, slots = ids_ref.shape
     centres = cent_ref.shape[0]
     half = rows.shape[2]
@@ -47,11 +48,29 @@
     other = {"rep": 1 - rep}
     far_first = sorted(range(1, holders), key=lambda k: -min(k, holders - k))
 
+    loads = [
+        pltpu.make_async_copy(src, dst, in_sem.at[i])
+        for i, (src, dst) in enumerate(
+            [
+                (ids_hbm, ids_ref),
+                (cent_hbm, cent_ref),
+                (q_hbm, q_all.at[0]),
+                (res_hbm, res_ref),
+                (len_hbm, len_ref),
+                (cand_hbm, cand_ref),
+            ]
+        )
+    ]
+    ids_load, cent_load, q_load, res_load, len_load, cand_load = loads
+    for load in loads:
+        load.start()
+
     barrier = pltpu.get_barrier_semaphore()
     for k in range(1, holders):
         pl.semaphore_signal(barrier, inc=1, device_id=at(k), device_id_type=MESH)
     pl.semaphore_signal(barrier, inc=1, device_id=other, device_id_type=MESH)
 
+    ids_load.wait()
     ids = ids_ref[...]
     target = ((ids >> log2(centres)) - me) & (holders - 1)
     local_id = ids & (centres - 1)
@@ -67,7 +86,9 @@
     rank = jnp.zeros((held, slots), F32)
     for k in range(holders):
         rank = rank + masks[k] * rank_all[k * held : (k + 1) * held]
-    slot_ref[...] = target.astype(F32) * (2.0 * half) + rank
+    later = jnp.where(rank >= half, 1.0, 0.0)
+    slot_ref[...] = target.astype(F32) * (1.0 * half) + rank - later * half
+    later_ref[...] = later
 
     low = (local_id & 255).astype(F32)
     high = (local_id >> 8).astype(F32)
@@ -86,7 +107,6 @@
     for k in range(1, holders):
         req_out[k] = jnp.broadcast_to(asked[k : k + 1], (8, half))
     req_in[0] = jnp.broadcast_to(asked[0:1], (8, half))
-    q_all[0] = q_ref[...]
     stat_out[...] = jnp.zeros_like(stat_out)
 
     pl.semaphore_wait(barrier, holders)
@@ -101,7 +121,7 @@
         return remote(req_out.at[k], req_in.at[k], r_send.at[k], r_recv.at[k], at(k))
 
     def q_copy(k):
-        return remote(q_ref, q_all.at[k], q_send.at[k], q_recv.at[k], at(k))
+        return remote(q_hbm, q_all.at[k], q_send.at[k], q_recv.at[k], at(k))
 
     def row_copy(k):
         return remote(found.at[k], rows.at[k, rep], f_send.at[k], f_recv.at[k], at(-k))
@@ -131,11 +151,26 @@
             [ones_where(spread - j * 128.0 == lanes.astype(F32)) for j in range(width // 128)], axis=1
         )
 
+    def choose(p, _):
+        here = pl.ds(p * slots, slots)
+        pick[here] = chosen(slot_ref[pl.ds(p, 1), :], half * holders)
+        later_all[here] = across(later_ref[pl.ds(p, 1), :])
+        return 0
+
+
+    middle = centres // 2
+    cent_load.wait()
+    wide_cent[:, 0:dim] = cent_ref[0:middle]
+    wide_cent[:, dim : 2 * dim] = cent_ref[middle:centres]
+
     for k in far_first + [0]:
         if k:
             req_copy(k).wait_recv()
-        hit = chosen(req_in[k][0:1].astype(F32), centres)
-        got = jnp.dot(hit, cent_ref[...], preferred_element_type=F32).astype(BF16)
+        name = req_in[k][0:1]
+        hit = chosen((name & (middle - 1)).astype(F32), middle)
+        both = jnp.dot(hit, wide_cent[...], preferred_element_type=F32)
+        upper = across((name >> log2(middle)).astype(F32)) > 0.5
+        got = jnp.where(upper, both[:, dim:], both[:, :dim]).astype(BF16)
         if k:
             found[k] = got
             row_copy(k).start()
@@ -145,6 +180,7 @@
 
     for k in far_first:
         q_copy(k).wait_recv()
+    q_load.wait()
     tokens = q_all[...].reshape(holders * qt, dim)
     best = None
     for j in range(centres // 256):
@@ -160,11 +196,6 @@
         jnp.where(own, best, 0.0), fold, precision=lax.Precision.HIGHEST, preferred_element_type=F32
     )
 
-    def choose(p, _):
-        row = slot_ref[pl.ds(p, 1), :]
-        pick[p] = chosen(row, 2 * half * holders)
-        return 0
-
     lax.fori_loop(0, held, choose, 0)
 
     near_first = far_first[::-1]
@@ -174,17 +205,23 @@
     for k in [0] + near_first:
         swap_arrival(k).wait_recv()
 
-    step = math.gcd(held, 4)
-    centre_rows = rows[...].reshape(holders * 2 * half, dim)
+    res_load.wait()
+    len_load.wait()
+    wide_rows = jnp.concatenate(
+        [rows[:, i].reshape(holders * half, dim) for i in range(2)], axis=1
+    )
+    tile = held * slots
     spot = iota((slots, width), 0)
-    for g in range(held // step):
-        group = pick[g * step : (g + 1) * step].reshape(step * slots, 2 * half * holders)
-        fetched = jnp.dot(group, centre_rows, preferred_element_type=F32)
-        residual = res_ref[g * step : (g + 1) * step].reshape(step * slots, dim).astype(F32)
+    for g in range(held * slots // tile):
+        here = slice(g * tile, (g + 1) * tile)
+        both = jnp.dot(pick[here], wide_rows, preferred_element_type=F32)
+        fetched = jnp.where(later_all[here] > 0.5, both[:, dim:], both[:, :dim])
+        first = g * tile // slots
+        residual = res_ref[first : first + tile // slots].reshape(tile, dim).astype(F32)
         decoded = (fetched + residual).astype(BF16)
         sims = lax.dot_general(decoded, tokens, NT, preferred_element_type=F32)
-        for i in range(step):
-            p = g * step + i
+        for i in range(tile // slots):
+            p = first + i
             live = jnp.where(spot < len_ref[p], sims[i * slots : (i + 1) * slots], -jnp.inf)
             pair_max[p : p + 1] = jnp.max(live, axis=0, keepdims=True)
     seg = jnp.where(own, 1.0, 0.0)
@@ -204,6 +241,7 @@
         maxima = jnp.maximum(maxima, stat_in[k][holders + k : holders + k + 1])
     best_ref[...] = maxima[:, 0:qt]
     table = jnp.concatenate(picked, axis=0)
+    cand_load.wait()
     cand = cand_ref[...]
     kc = cand.shape[1]
     where_p = jnp.where(iota((held, kc), 0) == (cand & (held - 1)), 1.0, 0.0)
@@ -228,6 +266,7 @@
     held, slots = centre_ids.shape
     half = held * slots // holders // 2
     vmem = pl.BlockSpec(memory_space=pltpu.VMEM)
+    hbm = pl.BlockSpec(memory_space=pltpu.HBM)
     dma = lambda: pltpu.SemaphoreType.DMA((holders,))
     return pl.pallas_call(
         functools.partial(fused_kernel, holders, lax.axis_size("cent")),
@@ -235,9 +274,15 @@
             jax.ShapeDtypeStruct((q_dev, qt), F32),
             jax.ShapeDtypeStruct((q_dev, candidates.shape[1]), F32),
         ),
-        in_specs=[vmem, vmem, vmem, vmem, pl.BlockSpec(memory_space=pltpu.SMEM), vmem],
+        in_specs=[hbm] * 6,
         out_specs=(vmem, vmem),
         scratch_shapes=[
+            pltpu.VMEM(candidates.shape, jnp.int32),
+            pltpu.VMEM(residuals.shape, BF16),
+            pltpu.VMEM(centre_ids.shape, jnp.int32),
+            pltpu.SMEM(lengths.shape, jnp.int32),
+            pltpu.VMEM(centroids.shape, BF16),
+            pltpu.SemaphoreType.DMA((6,)),
             pltpu.VMEM((holders, qt, dim), BF16),
             pltpu.VMEM((holders, 8, half), jnp.int32),
             pltpu.VMEM((holders, 8, half), jnp.int32),
@@ -246,12 +291,15 @@
             pltpu.VMEM((2 * holders, 128), F32),
             pltpu.VMEM((holders, 2 * holders, 128), F32),
             pltpu.VMEM((held, slots), F32),
-            pltpu.VMEM((held, slots, 2 * half * holders), BF16),
+            pltpu.VMEM((held, slots), F32),
+            pltpu.VMEM((held * slots, dim), F32),
+            pltpu.VMEM((held * slots, half * holders), BF16),
             pltpu.VMEM((held, holders * qt), F32),
+            pltpu.VMEM((centroids.shape[0] // 2, 2 * dim), BF16),
         ]
         + [dma() for _ in range(10)],
         compiler_params=pltpu.CompilerParams(
-            collective_id=0, has_side_effects=True, vmem_limit_bytes=40 * 1024 * 1024
+            collective_id=0, has_side_effects=True, vmem_limit_bytes=60 * 1024 * 1024
         ),
     )(queries.reshape(qt, dim), candidates, residuals, centre_ids, lengths, centroids)
 

time: 32.4 us -> 25.7 us (0.79)
  local copies, waits for them, and re-layouts: 5.15 us -> 1.8 us
  Pallas kernels: 26.3 us -> 23 us
    unnamed x14 -> x6, local copies, waits for them, and re-layouts: 5.15 us -> 1.8 us
    pallas_call x1, Pallas kernels: 26.3 us -> 23 us  [fused(): pl.pallas_call(functools.partial(fused_kernel, holders, lax.axis_size('ce...]
where the time goes in v2:
time: 25.7 us; the launch traced here: 25.5 us
  Pallas kernels  23 us (89%)
  local copies, waits for them, and re-layouts  1.8 us (7%)
  between operations  0.65 us (3%)
    pallas_call x1, Pallas kernels, fused(): pl.pallas_call(functools.partial(fused_kernel, holders, lax.axis_size('ce...  23 us
    unnamed x6, local copies, waits for them, and re-layouts  1.8 us

profile of v2, /device:TPU:0, one launch (start us, length us, event | category | flops | bytes accessed | tf_op | source)
XLA Modules:
  0.0 25.5 jit_solution(5814226069530887549)
XLA Ops:
  0.6 23.0 %shard_map.77 = (f32[1,32]{1,0:T(1,128)}, f32[1,64]{1,0:T(1,128)}) custom-call(bf16[32,128]{1,0:T(8,128)(2,1)} %bitcast.1, s32[1,64]{1,0:T(1,128)} %cand_hbm.1, bf16[16,128,128]{2,1,0:T(8,128)(2,1)} %res_hbm.1, s32[16,128]{1,0:T(8,128)} %ids_hbm.1, s32[16]{0:T(128)} %len_hbm.1, bf16[2048,128]{1,0:T(8,128)(2,1)} %cent_hbm.1), custom_call_target="tpu_custom_call" | custom-call | tf_op jit(solution)/shard_map/pallas_call | solution.py:271
  23.7 0.0 copy-start.1
  23.7 0.7 %copy-done.1 = f32[1,32]{1,0:T(1,128)S(1)} copy-done((f32[1,32]{1,0:T(1,128)S(1)}, f32[1,32]{1,0:T(1,128)}, u32[]{:S(2)}) %copy-start.1) | copy-done | bytes 152
  24.3 0.0 copy-start
  24.3 0.5 %copy.10 = f32[1,32]{1,0:T(1,128)} copy(f32[1,32]{1,0:T(1,128)S(1)} %copy-done.1) | data formatting | bytes 256
  24.8 0.1 copy-done
  25.0 0.5 %copy.11 = f32[1,64]{1,0:T(1,128)} copy(f32[1,64]{1,0:T(1,128)S(1)} %copy-done) | data formatting | bytes 512
Async XLA Ops:
  23.7 0.7 %copy-start.1 = (f32[1,32]{1,0:T(1,128)S(1)}, f32[1,32]{1,0:T(1,128)}, u32[]{:S(2)}) copy-start(f32[1,32]{1,0:T(1,128)} %get-tuple-element.4) | copy-start | bytes 388
  24.3 0.6 %copy-start = (f32[1,64]{1,0:T(1,128)S(1)}, f32[1,64]{1,0:T(1,128)}, u32[]{:S(2)}) copy-start(f32[1,64]{1,0:T(1,128)} %get-tuple-element.5) | copy-start | bytes 772

commit v3 on v2

--- a/solution.py
+++ b/solution.py
@@ -29,7 +29,7 @@
 def fused_kernel(
     holders, n_cent,
     q_hbm, cand_hbm, res_hbm, ids_hbm, len_hbm, cent_hbm,
-    best_ref, score_ref,
+    out_ref,
     cand_ref, res_ref, ids_ref, len_ref, cent_ref, in_sem,
     q_all, req_out, req_in, found, rows, stat_out, stat_in, slot_ref, later_ref, later_all, pick, pair_max, wide_cent,
     q_send, q_recv, r_send, r_recv, f_send, f_recv, x_send, x_recv, s_send, s_recv,
@@ -158,6 +158,8 @@
         return 0
 
 
+    lax.fori_loop(0, held // 2, choose, 0)
+
     middle = centres // 2
     cent_load.wait()
     wide_cent[:, 0:dim] = cent_ref[0:middle]
@@ -196,7 +198,7 @@
         jnp.where(own, best, 0.0), fold, precision=lax.Precision.HIGHEST, preferred_element_type=F32
     )
 
-    lax.fori_loop(0, held, choose, 0)
+    lax.fori_loop(held // 2, held, choose, 0)
 
     near_first = far_first[::-1]
     for k in near_first:
@@ -239,7 +241,7 @@
     maxima = stat_out[holders : holders + 1]
     for k in range(1, holders):
         maxima = jnp.maximum(maxima, stat_in[k][holders + k : holders + k + 1])
-    best_ref[...] = maxima[:, 0:qt]
+    out_ref[:, 0:qt] = maxima[:, 0:qt]
     table = jnp.concatenate(picked, axis=0)
     cand_load.wait()
     cand = cand_ref[...]
@@ -247,7 +249,7 @@
     where_p = jnp.where(iota((held, kc), 0) == (cand & (held - 1)), 1.0, 0.0)
     value = jnp.dot(table, where_p, precision=lax.Precision.HIGHEST, preferred_element_type=F32)
     holder = ((cand >> log2(held)) - me) & (holders - 1)
-    score_ref[...] = jnp.sum(
+    out_ref[:, qt : qt + kc] = jnp.sum(
         jnp.where(iota((holders, kc), 0) == holder, value, 0.0), axis=0, keepdims=True
     )
 
@@ -268,14 +270,11 @@
     vmem = pl.BlockSpec(memory_space=pltpu.VMEM)
     hbm = pl.BlockSpec(memory_space=pltpu.HBM)
     dma = lambda: pltpu.SemaphoreType.DMA((holders,))
-    return pl.pallas_call(
+    both = pl.pallas_call(
         functools.partial(fused_kernel, holders, lax.axis_size("cent")),
-        out_shape=(
-            jax.ShapeDtypeStruct((q_dev, qt), F32),
-            jax.ShapeDtypeStruct((q_dev, candidates.shape[1]), F32),
-        ),
+        out_shape=jax.ShapeDtypeStruct((q_dev, qt + candidates.shape[1]), F32),
         in_specs=[hbm] * 6,
-        out_specs=(vmem, vmem),
+        out_specs=vmem,
         scratch_shapes=[
             pltpu.VMEM(candidates.shape, jnp.int32),
             pltpu.VMEM(residuals.shape, BF16),
@@ -302,6 +301,7 @@
             collective_id=0, has_side_effects=True, vmem_limit_bytes=60 * 1024 * 1024
         ),
     )(queries.reshape(qt, dim), candidates, residuals, centre_ids, lengths, centroids)
+    return both[:, :qt], both[:, qt:]
 
 
 def fits(queries, residuals, centroids, holders, reps):

time: 25.7 us -> 25.6 us (level)
    unnamed x6 -> x3, local copies, waits for them, and re-layouts: 1.8 us -> 1.1 us
    slice x0 -> x1, local copies, waits for them, and re-layouts: none -> 0.58 us  [fused(): return (both[:, :qt], both[:, qt:])]
where the time goes in v3:
time: 25.6 us; the launch traced here: 25.3 us
  Pallas kernels  23 us (90%)
  local copies, waits for them, and re-layouts  1.68 us (7%)
  between operations  0.65 us (3%)
    pallas_call x1, Pallas kernels, fused(): pl.pallas_call(functools.partial(fused_kernel, holders, lax.axis_size('ce...  23 us
    unnamed x3, local copies, waits for them, and re-layouts  1.1 us
    slice x1, local copies, waits for them, and re-layouts, fused(): return (both[:, :qt], both[:, qt:])  0.58 us

profile of v3, /device:TPU:0, one launch (start us, length us, event | category | flops | bytes accessed | tf_op | source)
XLA Modules:
  0.0 25.3 jit_solution(9056947877389409018)
XLA Ops:
  0.6 23.0 %shard_map.77 = f32[1,96]{1,0:T(1,128)} custom-call(bf16[32,128]{1,0:T(8,128)(2,1)} %bitcast.2, s32[1,64]{1,0:T(1,128)} %cand_hbm.1, bf16[16,128,128]{2,1,0:T(8,128)(2,1)} %res_hbm.1, s32[16,128]{1,0:T(8,128)} %ids_hbm.1, s32[16]{0:T(128)} %len_hbm.1, bf16[2048,128]{1,0:T(8,128)(2,1)} %cent_hbm.1), custom_call_target="tpu_custom_call" | custom-call | tf_op jit(solution)/shard_map/pallas_call | solution.py:273
  23.6 0.0 copy-start
  23.7 0.6 %copy-done = f32[1,96]{1,0:T(1,128)S(1)} copy-done((f32[1,96]{1,0:T(1,128)S(1)}, f32[1,96]{1,0:T(1,128)}, u32[]{:S(2)}) %copy-start) | copy-done | bytes 408
  24.2 0.6 %slice.7 = f32[1,64]{1,0:T(1,128)} slice(f32[1,96]{1,0:T(1,128)S(1)} %copy-done), slice={[0:1], [32:96]} | slice | bytes 512 | tf_op jit(solution)/shard_map/slice | solution.py:304
  24.8 0.5 %copy.9 = f32[1,32]{1,0:T(1,128)} copy(f32[1,32]{1,0:T(1,128)S(1)} %bitcast.3) | data formatting | bytes 256
Async XLA Ops:
  23.6 0.6 %copy-start = (f32[1,96]{1,0:T(1,128)S(1)}, f32[1,96]{1,0:T(1,128)}, u32[]{:S(2)}) copy-start(f32[1,96]{1,0:T(1,128)} %shard_map.77) | copy-start | bytes 1156
